TPU v7x, 32 devices: a whole 2x2x4 slice. The times are simulated.
32 devices in a mesh: space: 16 (over z, x, core), ky: 2 (over y).
Axes of the slice: x: 2, y: 2, z: 4, core: 2. Of those that a mesh axis runs over, the one named last changes fastest.
Arguments:
- distribution: float32 [16, 128, 256, 128], P('space', 'ky'), may hold values from 0 to 2
- region: int32 [16, 256], P('space'), may hold values from 0 to 5, as said below
- region_doping: float32 [6], replicated, may hold values from -1 to 2
- region_relax: float32 [6], replicated, may hold values from 0.2 to 1
- equilibrium: float32 [128, 128], P('ky'), may hold values from 0.3 to 3
- kx_speed: float32 [128], replicated, may hold values from 0.1 to 1
- upwind_sign: int32 [128], replicated, may hold values from -1 to 1, as said below
Outputs:
- advanced: float32 [16, 128, 256, 128], P('space', 'ky')
Inputs may be any that keep to these rules, and one draw needn't show every extreme that they name: region[x, y] = 2 band(y) + m[x, y], with m[x, y] 0 or 1 and band(y) = 0, 1, 2 on three runs of columns, each run at least 32 columns long. `upwind_sign`: exactly 64 entries are 1 and the others -1.
All inputs are finite; a program needn't handle non-finite values.
Results may differ from a plain program's by a relative error of at most 0.0003.
Values sent between devices are 32-bit elements; how exact they have to be, the bound alone decides.
A program may use at most 128 MiB of HBM per device.

v0:
```python
import math

import jax
import jax.numpy as jnp
from jax import lax
from jax.sharding import PartitionSpec as P

COUPLING = 0.04
POISSON = 0.1
STEP = 0.4
DRIFT_Y = 0.8


def with_halo(block, sides, width):
    for axis, dim in sides:
        count = lax.axis_size(axis)
        forward = [(i, i + 1) for i in range(count - 1)]
        backward = [(target, source) for source, target in forward]
        low = lax.ppermute(
            lax.slice_in_dim(block, block.shape[dim] - width, None, axis=dim), axis, forward
        )
        high = lax.ppermute(lax.slice_in_dim(block, 0, width, axis=dim), axis, backward)
        block = jnp.concatenate([low, block, high], axis=dim)
    return block


def sine_table(length):
    positions = jnp.arange(1, length + 1, dtype=jnp.int32)
    phase_index = positions[:, None] * positions[None, :] % (2 * length + 2)
    return jnp.sqrt(2.0 / (length + 1.0)) * jnp.sin(
        math.pi * phase_index.astype(jnp.float32) / (length + 1.0)
    )


def eigen_values(length):
    positions = jnp.arange(1, length + 1, dtype=jnp.int32).astype(jnp.float32)
    return 4.0 * jnp.sin(0.5 * math.pi * positions / (length + 1.0)) ** 2


def wigner_tables(modes):
    half_count = modes // 2
    shifts = jnp.arange(1, half_count + 1, dtype=jnp.int32)
    wave_index = jnp.arange(modes, dtype=jnp.int32)
    phase_index = shifts[:, None] * wave_index[None, :] % modes
    angles = 2.0 * math.pi / modes * phase_index.astype(jnp.float32)
    forward = jnp.concatenate([jnp.cos(angles), jnp.sin(angles)], axis=0)
    backward = jnp.concatenate([jnp.sin(angles).T, -jnp.cos(angles).T], axis=1)
    return (forward, backward)


def own_differences(potential, modes, first_col, local_cols):
    half_count = modes // 2
    padded = jnp.pad(potential, ((0, 0), (half_count, half_count)))
    window = lax.dynamic_slice_in_dim(padded, first_col, local_cols + 2 * half_count, 1)
    pieces = []
    for offset in range(1, half_count + 1):
        ahead_vals = window[:, half_count + offset : half_count + offset + local_cols]
        behind = window[:, half_count - offset : half_count - offset + local_cols]
        pieces.append(ahead_vals - behind)
    return COUPLING * jnp.stack(pieces, axis=1)


def lookup(region, values_table):
    classes = jnp.arange(values_table.shape[0], dtype=jnp.int32)
    return jnp.sum(jnp.where(region[..., None] == classes, values_table, 0.0), axis=-1)


def shards(distribution, region, region_doping, region_relax, equilibrium, kx_speed, upwind_sign):
    precise = lax.Precision.HIGHEST
    triple = lax.Precision.HIGH
    row_count, ky_local, col_count, kx_count = distribution.shape
    ky_count = ky_local * lax.axis_size("ky")
    grid_rows = row_count * lax.axis_size("space")
    row_start = lax.axis_index("space") * row_count
    partial_value = jnp.sum(distribution, axis=(1, 3)) / (ky_count * kx_count)
    density = lax.psum(partial_value, "ky")
    doping = lookup(region, region_doping)
    relax_rate = lookup(region, region_relax)
    charge = density - doping
    sine_rows = sine_table(grid_rows)
    sine_cols = sine_table(col_count)
    eigen_cols = eigen_values(col_count)
    every_row = lax.all_gather(charge, "space", axis=0, tiled=True)
    along_x = jnp.dot(sine_rows, every_row, precision=precise)
    spectral = jnp.dot(along_x, sine_cols, precision=precise)
    spectral = spectral / (eigen_values(grid_rows)[:, None] + eigen_cols[None, :])
    back_cols = jnp.dot(spectral, sine_cols, precision=precise)
    own_rows = lax.dynamic_slice_in_dim(sine_rows, row_start, row_count, 0)
    potential = POISSON * jnp.dot(own_rows, back_cols, precision=precise)
    spread = lax.all_to_all(distribution, "ky", split_axis=2, concat_axis=1, tiled=True)
    local_cols = spread.shape[2]
    forward, backward = wigner_tables(ky_count)
    weights = own_differences(potential, ky_count, lax.axis_index("ky") * local_cols, local_cols)
    flattened = spread.reshape(row_count, ky_count, local_cols * kx_count)
    coeffs = jnp.einsum("ab,rbm->ram", forward, flattened, precision=triple)
    coeffs = coeffs.reshape(row_count, ky_count, local_cols, kx_count)
    scaled = coeffs * jnp.concatenate([weights, weights], axis=1)[..., None]
    mixed = jnp.einsum(
        "ab,rbm->ram",
        backward,
        scaled.reshape(row_count, ky_count, local_cols * kx_count),
        precision=triple,
    )
    mixed = mixed.reshape(row_count, ky_count, local_cols, kx_count)
    wigner = lax.all_to_all(mixed, "ky", split_axis=1, concat_axis=2, tiled=True)
    positive_kx = upwind_sign > 0
    padded = with_halo(distribution, (("space", 0),), 1)
    from_left = padded[:-2]
    from_right = padded[2:]
    upstream_x = jnp.where(positive_kx[None, None, None, :], from_left, from_right)
    drift_x = -kx_speed[None, None, None, :] * (distribution - upstream_x)
    ky_global = lax.axis_index("ky") * ky_local + jnp.arange(ky_local, dtype=jnp.int32)
    upward = ky_global >= ky_count // 2
    vertical = DRIFT_Y * (ky_global.astype(jnp.float32) + 0.5 - 0.5 * ky_count) / (0.5 * ky_count)
    zero_col = jnp.zeros_like(distribution[:, :, :1])
    from_low = jnp.concatenate([zero_col, distribution[:, :, :-1]], axis=2)
    from_high = jnp.concatenate([distribution[:, :, 1:], zero_col], axis=2)
    upstream_y = jnp.where(upward[None, :, None, None], from_low, from_high)
    drift_y = -jnp.abs(vertical)[None, :, None, None] * (distribution - upstream_y)
    relaxation = relax_rate[:, None, :, None] * (
        density[:, None, :, None] * equilibrium[None, :, None, :] - distribution
    )
    return distribution + STEP * (drift_x + drift_y + wigner + relaxation)


def solution(mesh):
    return jax.shard_map(
        shards,
        mesh=mesh,
        in_specs=(
            P("space", "ky", None, None),
            P("space", None),
            P(),
            P(),
            P("ky", None),
            P(),
            P(),
        ),
        out_specs=P("space", "ky", None, None),
        check_vma=False,
    )
```

profile of v0, /device:TPU:0, one launch (start us, length us, event | category | flops | bytes accessed | tf_op | source)
XLA Modules:
  0.0 389.2 jit_solution(937371054188645448)
XLA Ops:
  0.0 1.3 collective-permute-start.1
  1.3 6.3 %collective-permute-start = (f32[1,64,256,128]{3,2,1,0:T(8,128)}, f32[1,64,256,128]{3,2,1,0:T(8,128)}, u32[]{:S(2)}, u32[]{:S(2)}) collective-permute-start(f32[1,64,256,128]{3,2,1,0:T(8,128)} %param.7), channel_id=1, source_target_pairs={{0,2},{2,4},{4,6},{6,8},{8,10},{10,12},{12,14},{14,16},{16,18},{18... | collective-permute-start | bytes 25165832 | tf_op jit(solution)/shard_map/ppermute | solution.py:19
  7.6 11.5 %copy.18 = f32[1,64,256,128]{3,1,0,2:T(8,128)} copy(f32[1,64,256,128]{3,2,1,0:T(8,128)} %param.7) | data formatting | bytes 16777216 | tf_op args[0]
  19.1 6.9 %all-to-all-start = ((f32[1,64,256,128]{3,1,0,2:T(8,128)}), f32[1,64,256,128]{3,1,0,2:T(8,128)}, u32[]{:S(2)}, u32[]{:S(2)}) async-start(f32[1,64,256,128]{3,1,0,2:T(8,128)} %copy.18), calls=%async_computation | async-start | bytes 16777216 | tf_op jit(solution)/shard_map/all_to_all | solution.py:90
  26.1 3.9 reduce_sum.29
  29.9 88.2 %psum.7 = f32[1,256]{1,0:T(1,128)S(1)} all-reduce(f32[1,256]{1,0:T(1,128)S(1)} %bitcast.205), channel_id=1, replica_groups=mesh['space'=16,'ky'=2] {'ky'}, use_global_device_ids=true, to_apply=%region_1.0 | all-reduce | flops 256 | bytes 2048 | tf_op jit(solution)/shard_map/psum | solution.py:76
  118.3 78.3 %all-gather = f32[16,1,256]{2,1,0:T(1,128)S(1)} all-gather(f32[1,1,256]{2,1,0:T(1,128)S(1)} %subtract_bitcast_fusion), channel_id=1, replica_groups=mesh['space'=16,'ky'=2] {'space'}, dimensions={0}, use_global_device_ids=true | all-gather | bytes 17408 | tf_op jit(solution)/shard_map/all_gather | solution.py:83
  196.8 0.3 fusion.51
  197.0 1.3 convolution_divide_fusion
  198.3 1.3 fusion.14
  201.7 0.2 stack.259
  202.0 4.7 %mul.259 = f32[128,128,128]{2,1,0:T(8,128)} broadcast(f32[128,128]{1,0:T(8,128)S(1)} %maximum_bitcast_fusion), dimensions={0,1} | broadcast | bytes 8454144 | tf_op jit(solution)/shard_map/mul | solution.py:97
  206.7 9.4 %mul.260 = f32[1,128,16384]{2,1,0:T(8,128)} reshape(f32[128,128,128]{2,1,0:T(8,128)} %mul.259) | data formatting | bytes 16777216 | tf_op jit(solution)/shard_map/mul | solution.py:97
  216.1 0.2 fusion.55
  216.3 0.3 fusion.47
  216.6 11.8 %copy.19 = f32[1,64,2,128,128]{4,3,1,2,0:T(8,128)} copy(f32[1,64,2,128,128]{4,1,3,2,0:T(8,128)} %bitcast) | data formatting | bytes 16777216 | tf_op jit(solution)/shard_map/all_to_all | solution.py:90
  228.4 12.0 %fusion.1 = f32[128,16384]{1,0:T(8,128)S(1)} fusion(f32[1,128,16384]{2,1,0:T(8,128)S(1)} %copy-done, f32[16,8,128,128]{3,2,1,0:T(8,128)} %bitcast.185, f32[64,128]{1,0:T(8,128)S(1)} %get-tuple-element.76, f32[64,128]{1,0:T(8,128)S(1)} %get-tuple-element.75), kind=kOutput, calls=%fused_computation.2 | convolution fusion | flops 1612726272 | bytes 25231360 | tf_op jit(solution)/shard_map/ab,rbm->ram/dot_general | solution.py:95
  240.4 9.4 %fusion.35 = f32[16384,128]{1,0:T(8,128)} fusion(f32[128,16384]{1,0:T(8,128)S(1)} %fusion.1, f32[128,64]{1,0:T(8,128)S(1)} %get-tuple-element.74, f32[128,64]{1,0:T(8,128)S(1)} %get-tuple-element.73), kind=kOutput, calls=%fused_computation.42 | convolution fusion | flops 1610629120 | bytes 16842752 | tf_op jit(solution)/shard_map/ab,rbm->ram/dot_general | solution.py:98
  249.8 9.3 %copy.20 = f32[1,128,128,128]{3,2,0,1:T(8,128)} copy(f32[1,128,128,128]{1,3,2,0:T(8,128)} %bitcast.184) | data formatting | bytes 16777216 | tf_op jit(solution)/shard_map/reshape | solution.py:104
  259.1 7.1 %all-to-all-start.1 = ((f32[1,128,128,128]{3,2,0,1:T(8,128)}), f32[1,128,128,128]{3,2,0,1:T(8,128)}, u32[]{:S(2)}, u32[]{:S(2)}) async-start(f32[1,128,128,128]{3,2,0,1:T(8,128)} %copy.20), calls=%async_computation.1 | async-start | bytes 16777216 | tf_op jit(solution)/shard_map/all_to_all | solution.py:105
  266.2 12.8 %fusion.209 = (f32[1,64,255,128]{3,2,1,0:T(8,128)}, f32[1,64,255,128]{3,2,1,0:T(8,128)}) fusion(f32[1,64,256,128]{3,2,1,0:T(8,128)} %param.7), kind=kLoop, calls=%fused_computation.363 | loop fusion | bytes 33423360 | tf_op jit(solution)/shard_map/slice | solution.py:116
  279.0 80.1 %all-to-all-done.1 = f32[1,128,128,128]{3,2,0,1:T(8,128)} async-done(((f32[1,128,128,128]{3,2,0,1:T(8,128)}), f32[1,128,128,128]{3,2,0,1:T(8,128)}, u32[]{:S(2)}, u32[]{:S(2)}) %all-to-all-start.1) | async-done | bytes 8388640 | tf_op jit(solution)/shard_map/all_to_all | solution.py:105
  359.1 7.7 %copy.21 = f32[1,64,2,128,128]{4,3,2,1,0:T(8,128)} copy(f32[1,64,2,128,128]{4,3,1,2,0:T(8,128)} %bitcast.83) | data formatting | bytes 16777216 | tf_op jit(solution)/shard_map/all_to_all | solution.py:105
  366.9 22.3 %fusion.6 = f32[1,64,256,128]{3,2,1,0:T(8,128)} fusion(f32[1,64,256,128]{3,2,1,0:T(8,128)} %param.7, f32[1,64,2,128,128]{4,3,2,1,0:T(8,128)} %copy.21, f32[1,64,255,128]{3,2,1,0:T(8,128)} %get-tuple-element.8, f32[1,64,255,128]{3,2,1,0:T(8,128)} %get-tuple-element.7, f32[1,64,256,128]{3,2,1,0:T(8,128)} %collective-permute-done, ...), kind=kLoop, calls=%fused_computation.8 | loop fusion | flops 29360128 | bytes 58690496 | tf_op jit(solution)/shard_map/add | solution.py:123
  (50 shorter events, 2.5 us)
Async XLA Ops:
  0.0 366.9 %collective-permute-start.1 = (f32[1,64,256,128]{3,2,1,0:T(8,128)}, f32[1,64,256,128]{3,2,1,0:T(8,128)}, u32[]{:S(2)}, u32[]{:S(2)}) collective-permute-start(f32[1,64,256,128]{3,2,1,0:T(8,128)} %param.7), channel_id=1, source_target_pairs={{2,0},{4,2},{6,4},{8,6},{10,8},{12,10},{14,12},{16,14},{18,16},{20... | collective-permute-start | bytes 25165832 | tf_op jit(solution)/shard_map/ppermute | solution.py:22
  1.3 365.6 %collective-permute-start = (f32[1,64,256,128]{3,2,1,0:T(8,128)}, f32[1,64,256,128]{3,2,1,0:T(8,128)}, u32[]{:S(2)}, u32[]{:S(2)}) collective-permute-start(f32[1,64,256,128]{3,2,1,0:T(8,128)} %param.7), channel_id=1, source_target_pairs={{0,2},{2,4},{4,6},{6,8},{8,10},{10,12},{12,14},{14,16},{16,18},{18... | collective-permute-start | bytes 25165832 | tf_op jit(solution)/shard_map/ppermute | solution.py:19
  19.1 197.5 %all-to-all-start = ((f32[1,64,256,128]{3,1,0,2:T(8,128)}), f32[1,64,256,128]{3,1,0,2:T(8,128)}, u32[]{:S(2)}, u32[]{:S(2)}) async-start(f32[1,64,256,128]{3,1,0,2:T(8,128)} %copy.18), calls=%async_computation | async-start | bytes 16777216 | tf_op jit(solution)/shard_map/all_to_all | solution.py:90
  26.0 92.2 %copy-start.2 = (s32[1,256]{1,0:T(1,128)S(1)}, s32[1,256]{1,0:T(1,128)}, u32[]{:S(2)}) copy-start(s32[1,256]{1,0:T(1,128)} %param.8) | copy-start | bytes 3076
  26.0 92.1 %copy-start.3 = (f32[6]{0:T(128)S(1)}, f32[6]{0:T(128)}, u32[]{:S(2)}) copy-start(f32[6]{0:T(128)} %param.10) | copy-start | bytes 76
  26.0 92.1 %copy-start.4 = (f32[6]{0:T(128)S(1)}, f32[6]{0:T(128)}, u32[]{:S(2)}) copy-start(f32[6]{0:T(128)} %param.9) | copy-start | bytes 76
  216.6 11.8 %copy-start = (f32[1,128,16384]{2,1,0:T(8,128)S(1)}, f32[1,128,16384]{2,1,0:T(8,128)}, u32[]{:S(2)}) copy-start(f32[1,128,16384]{2,1,0:T(8,128)} %mul.260) | copy-start | bytes 25165828
  259.1 7.1 %copy-start.5 = (f32[128]{0:T(128)S(1)}, f32[128]{0:T(128)}, u32[]{:S(2)}) copy-start(f32[128]{0:T(128)} %param.12) | copy-start | bytes 1540
  259.1 7.1 %copy-start.6 = (s32[128]{0:T(128)S(1)}, s32[128]{0:T(128)}, u32[]{:S(2)}) copy-start(s32[128]{0:T(128)} %param.13) | copy-start | bytes 1540
  259.1 100.0 %all-to-all-start.1 = ((f32[1,128,128,128]{3,2,0,1:T(8,128)}), f32[1,128,128,128]{3,2,0,1:T(8,128)}, u32[]{:S(2)}, u32[]{:S(2)}) async-start(f32[1,128,128,128]{3,2,0,1:T(8,128)} %copy.20), calls=%async_computation.1 | async-start | bytes 16777216 | tf_op jit(solution)/shard_map/all_to_all | solution.py:105
  359.1 7.7 %copy-start.1 = (f32[64,128]{1,0:T(8,128)S(1)}, f32[64,128]{1,0:T(8,128)}, u32[]{:S(2)}) copy-start(f32[64,128]{1,0:T(8,128)} %param.11) | copy-start | bytes 98308
where the time goes:
time: 390 us; the launch traced here: 389 us
  blocking collectives  166 us (43%)
  waiting for transfers between devices  80.1 us (21%)
  local copies, waits for them, and re-layouts  67.5 us (17%)
  other arithmetic  29 us (7%)
  matrix products  24.4 us (6%)
  starting transfers between devices  21.6 us (6%)
    psum x1, blocking collectives, shards(): density = lax.psum(partial_value, 'ky')  88.2 us
    all_to_all x1, waiting for transfers between devices, shards(): lax.all_to_all(mixed, 'ky', split_axis=1, concat_axis=2, tiled=True)  80.1 us
    all_gather x1, blocking collectives, shards(): every_row = lax.all_gather(charge, 'space', axis=0, tiled=True)  78.3 us
    add x1, other arithmetic, shards(): return distribution + STEP * (drift_x + drift_y + wigner + relaxation)  22.3 us
    mul x2, local copies, waits for them, and re-layouts, shards(): scaled = coeffs * jnp.concatenate([weights, weights], axis=1)[..., None]  14.1 us
    slice x1, local copies, waits for them, and re-layouts, shards(): from_low = jnp.concatenate([zero_col, distribution[:, :, :-1]], axis=2)  12.8 us
    dot_general x1, matrix products, shards(): coeffs = jnp.einsum('ab,rbm->ram', forward, flattened, precision=triple)  12 us
    all_to_all x1, local copies, waits for them, and re-layouts, shards(): lax.all_to_all(distribution, 'ky', split_axis=2, concat_axis=1, tiled=True)  11.8 us
  transfers between devices with their start and end apart: 4, of which 1 were waited for; matrix products, arithmetic and copies ran while one was open for 25% of the time, Pallas kernels for 0%

commit v1 on v0

v1 whole, which is shorter than its diff:
```python
import functools

import jax
import jax.numpy as jnp
import numpy as np
from jax import lax
from jax.experimental import pallas as pl
from jax.experimental.pallas import tpu as pltpu
from jax.sharding import PartitionSpec as P

COUPLING = 0.04
POISSON = 0.1
STEP = 0.4
DRIFT_Y = 0.8
WIDTH = 16
HALF = WIDTH // 2
EARLY = 2
MESH = pl.DeviceIdType.MESH
BF16 = jnp.bfloat16
F32 = jnp.float32


def sine_table(length):
    positions = np.arange(1, length + 1)
    phase = positions[:, None] * positions[None, :] % (2 * length + 2)
    return np.sqrt(2.0 / (length + 1.0)) * np.sin(np.pi * phase / (length + 1.0))


def eigen_values(length):
    positions = np.arange(1, length + 1)
    return 4.0 * np.sin(0.5 * np.pi * positions / (length + 1.0)) ** 2


def tables(rows, groups, modes, cols):
    half = modes // 2
    local = modes // groups
    phase = np.arange(1, half + 1)[:, None] * np.arange(modes)[None, :] % modes
    angles = 2.0 * np.pi / modes * phase
    forward = np.concatenate([np.cos(angles), np.sin(angles)], axis=0)
    backward = np.concatenate([np.sin(angles).T, -np.cos(angles).T], axis=1)
    by_owner = forward.reshape(modes, groups, local)
    forward_of = np.stack(
        [
            np.concatenate([by_owner[:, (g - p) % groups] for p in range(groups)], axis=1)
            for g in range(groups)
        ]
    )
    backward_of = backward.reshape(groups, local, modes)
    speed = DRIFT_Y * (np.arange(modes) + 0.5 - 0.5 * modes) / (0.5 * modes)
    speed_of = np.broadcast_to(speed.reshape(groups, local, 1), (groups, local, 128))
    sine_rows = sine_table(rows)
    expand = np.zeros((rows, rows, 8))
    expand[:, :, 0] = sine_rows
    own_row = np.broadcast_to(sine_rows[:, None, :], (rows, 8, rows))
    sine_cols = sine_table(cols)
    padded = np.pad(sine_cols, ((0, 0), (half, half)))
    pick = np.zeros((cols + 2 * half, 2 * half))
    centre = cols - 1 + half
    for s in range(1, half + 1):
        for column in (s - 1, half + s - 1):
            pick[centre + s, column] = 1.0
            pick[centre - s, column] = -1.0
    eigen = eigen_values(rows)[:, None] + eigen_values(cols)[None, :]
    every = (
        forward_of, backward_of, speed_of, expand.reshape(rows, rows * 8), own_row,
        sine_cols, padded, pick, eigen,
    )
    return [np.asarray(t, np.float32) for t in every]


def exact(a, b, contract=((1,), (0,))):
    return lax.dot_general(
        a, b, (contract, ((), ())), precision=lax.Precision.HIGHEST, preferred_element_type=F32
    )


def split(x):
    high = x.astype(BF16)
    return high, (x - high.astype(F32)).astype(BF16)


def triple(a, b):
    (a_high, a_low), (b_high, b_low) = a, b
    mul = functools.partial(jnp.dot, preferred_element_type=F32)
    return mul(a_high, b_high) + (mul(a_high, b_low) + mul(a_low, b_high))


def kernel(
    rows, groups,
    f_hbm, region_ref, doping_ref, relax_ref, eq_ref, speed_ref, sign_ref,
    forward_ref, backward_ref, vertical_ref, expand_ref, own_row_ref,
    sine_ref, padded_ref, pick_ref, eigen_ref,
    out_hbm,
    f_vm, spread, to_left, to_right, from_left, from_right, weight_high, weight_low,
    sums, parts, charges, diffs, dens, rate, up_x, result,
    load_sem, spread_send, spread_recv, part_send, part_recv, charge_send, charge_recv,
    left_send, left_recv, right_send, right_recv, out_sem,
):
    _, local, cols, kx = f_hbm.shape
    modes = local * groups
    chunks = cols // WIDTH
    row = lax.axis_index("space")
    group = lax.axis_index("ky")

    def other_group(p):
        return (row, lax.rem(group + p, groups))

    def other_row(i):
        return (lax.rem(row + i, rows), group)

    barrier = pltpu.get_barrier_semaphore()
    for p in range(1, groups):
        pl.semaphore_signal(barrier, inc=1, device_id=other_group(p), device_id_type=MESH)

    @pl.loop(1, rows)
    def _(i):
        pl.semaphore_signal(barrier, inc=1, device_id=other_row(i), device_id_type=MESH)

    def load(c):
        return pltpu.make_async_copy(
            f_hbm.at[0, :, pl.ds(pl.multiple_of(c * WIDTH, WIDTH), WIDTH), :],
            f_vm.at[c + 1], load_sem.at[c],
        )

    @pl.loop(0, chunks)
    def _(c):
        load(c).start()

    pl.semaphore_wait(barrier, rows + groups - 2)

    def spread_copy(p, c):
        return pltpu.make_async_remote_copy(
            src_ref=f_hbm.at[0, :, pl.ds(pl.multiple_of(c * WIDTH, WIDTH), WIDTH), :],
            dst_ref=spread.at[p - 1, c],
            send_sem=spread_send.at[p - 1, c], recv_sem=spread_recv.at[p - 1, c],
            device_id=other_group(p), device_id_type=MESH,
        )

    def part_copy(p):
        return pltpu.make_async_remote_copy(
            src_ref=parts.at[0], dst_ref=parts.at[p],
            send_sem=part_send.at[p - 1], recv_sem=part_recv.at[p - 1],
            device_id=other_group(p), device_id_type=MESH,
        )

    def charge_copy(i):
        return pltpu.make_async_remote_copy(
            src_ref=charges.at[0], dst_ref=charges.at[i],
            send_sem=charge_send.at[i - 1], recv_sem=charge_recv.at[i - 1],
            device_id=other_row(i), device_id_type=MESH,
        )

    def right_copy(c):
        return pltpu.make_async_remote_copy(
            src_ref=to_right.at[c], dst_ref=from_left.at[c],
            send_sem=right_send.at[c], recv_sem=right_recv.at[c],
            device_id=other_row(1), device_id_type=MESH,
        )

    def left_copy(c):
        return pltpu.make_async_remote_copy(
            src_ref=to_left.at[c], dst_ref=from_right.at[c],
            send_sem=left_send.at[c], recv_sem=left_recv.at[c],
            device_id=other_row(rows - 1), device_id_type=MESH,
        )

    for c in range(min(EARLY, chunks)):
        for p in range(1, groups):
            spread_copy(p, c).start()

    blank = jnp.zeros(f_vm.shape[1:], F32)
    f_vm[0] = blank
    f_vm[chunks + 1] = blank

    @pl.loop(0, chunks)
    def _(c):
        load(c).wait()
        sums[pl.ds(pl.multiple_of(c * WIDTH, WIDTH), WIDTH), :] = jnp.sum(f_vm[c + 1], axis=0)

    parts[0] = exact(jnp.ones((8, kx), F32), sums[...], ((1,), (1,))) / (modes * kx)
    for p in range(1, groups):
        part_copy(p).start()

    @pl.loop(min(EARLY, chunks), chunks)
    def _(c):
        for p in range(1, groups):
            spread_copy(p, c).start()

    lane = lax.broadcasted_iota(jnp.int32, (kx, kx), 1)
    place = lax.broadcasted_iota(jnp.int32, (kx, kx), 0)
    positive = jnp.broadcast_to(sign_ref[...] > 0, (kx, kx))
    ahead = exact(positive.astype(F32), (place < lane).astype(F32)).astype(jnp.int32)
    target = jnp.where(positive, ahead, kx // 2 + lane - ahead)
    first = (target == place).astype(F32)
    second = (lax.rem(target + kx // 2, kx) == place).astype(F32)
    low_lane = lax.broadcasted_iota(jnp.int32, (local * HALF, kx), 1) < kx // 2

    @pl.loop(0, chunks)
    def _(c):
        one = exact(f_vm[c + 1, :, :HALF, :].reshape(local * HALF, kx), first, ((1,), (1,)))
        two = exact(f_vm[c + 1, :, HALF:, :].reshape(local * HALF, kx), second, ((1,), (1,)))
        to_right[c] = jnp.where(low_lane, one, two).reshape(local, HALF, kx)
        to_left[c] = jnp.where(low_lane, two, one).reshape(local, HALF, kx)

    def lookup(table):
        region = jnp.broadcast_to(region_ref[...], (8, cols))
        value = jnp.zeros((8, cols), F32)
        for k in range(table.shape[0]):
            value = value + jnp.where(region == k, table[k], 0.0)
        return value

    def down(values):
        shape = (cols, cols)
        same = lax.broadcasted_iota(jnp.int32, shape, 0) == lax.broadcasted_iota(jnp.int32, shape, 1)
        spread_out = jnp.where(same, jnp.broadcast_to(values[:1], shape), 0.0)
        return exact(spread_out, jnp.ones((cols, kx), F32))

    rate[...] = down(lookup(relax_ref))
    for p in range(1, groups):
        part_copy(p).wait_recv()
    density = parts[0]
    for p in range(1, groups):
        density = density + parts[p]
    charges[0] = density - lookup(doping_ref)

    @pl.loop(1, rows)
    def _(i):
        charge_copy(i).start()

    @pl.loop(0, chunks)
    def _(c):
        @pl.when(row < rows - 1)
        def _():
            right_copy(c).start()

        @pl.when(row > 0)
        def _():
            left_copy(c).start()

    @pl.when(row == 0)
    def _():
        @pl.loop(0, chunks)
        def _(c):
            from_left[c] = jnp.zeros(from_left.shape[1:], F32)

    @pl.when(row == rows - 1)
    def _():
        @pl.loop(0, chunks)
        def _(c):
            from_right[c] = jnp.zeros(from_right.shape[1:], F32)

    dens[...] = down(density)

    @pl.loop(1, rows)
    def _(i):
        charge_copy(i).wait_recv()

    along_x = exact(expand_ref[row], charges[...].reshape(rows * 8, cols))
    spectral = exact(along_x, sine_ref[...]) / eigen_ref[...]
    own = exact(own_row_ref[row], spectral)
    potential = POISSON * exact(own, padded_ref[...])
    wide = jnp.broadcast_to(potential[:1], (cols, potential.shape[1]))
    shifted = pltpu.roll(wide, 0, 1, stride=1, stride_axis=0)
    diffs[...] = COUPLING * exact(shifted, pick_ref[...])

    forward = split(forward_ref[group])

    @pl.loop(0, chunks)
    def _(c):
        scaled = []
        for j in range(WIDTH):
            weights = diffs[pl.ds(cols - 1 - (c * WIDTH + j), 1), :]
            scaled.append(backward_ref[group] * weights)
        table = triple(split(jnp.concatenate(scaled, axis=0)), forward)
        high, low = split(table)
        weight_high[c] = high
        weight_low[c] = low

    f_rows = f_vm.reshape((chunks + 2) * local * WIDTH, kx)
    spread_rows = spread.reshape((groups - 1) * chunks * local * WIDTH, kx)
    up_rows = up_x.reshape(2 * local * HALF, kx)
    result_rows = result.reshape(2 * local * WIDTH, kx)

    def own_column(c, j):
        c, j = (c - 1, WIDTH - 1) if j < 0 else (c + 1, 0) if j == WIDTH else (c, j)
        return f_rows[pl.ds((c + 1) * (local * WIDTH) + j, local, stride=WIDTH), :]

    def out_copy(c):
        slot = lax.rem(c, 2)
        return pltpu.make_async_copy(
            result.at[slot],
            out_hbm.at[0, :, pl.ds(pl.multiple_of(c * WIDTH, WIDTH), WIDTH), :],
            out_sem.at[slot],
        )

    @pl.loop(0, chunks)
    def _(c):
        @pl.when(row > 0)
        def _():
            right_copy(c).wait_recv()

        @pl.when(row < rows - 1)
        def _():
            left_copy(c).wait_recv()

        left = from_left[c].reshape(local * HALF, kx)
        right = from_right[c].reshape(local * HALF, kx)
        up_x[0] = exact(jnp.where(low_lane, left, right), first).reshape(local, HALF, kx)
        up_x[1] = exact(jnp.where(low_lane, right, left), second).reshape(local, HALF, kx)

        @pl.when(c >= 2)
        def _():
            out_copy(c - 2).wait()

        for p in range(1, groups):
            spread_copy(p, c).wait_recv()

        vertical = vertical_ref[group]
        for j in range(WIDTH):
            current = own_column(c, j)
            every = [current]
            for p in range(groups - 1):
                start = (p * chunks + c) * (local * WIDTH) + j
                every.append(spread_rows[pl.ds(start, local, stride=WIDTH), :])
            picked = pl.ds(j * local, local)
            wigner = triple(
                (weight_high[c, picked, :], weight_low[c, picked, :]),
                split(jnp.concatenate(every, axis=0)),
            )
            half, inner = divmod(j, HALF)
            upstream_x = up_rows[pl.ds(half * local * HALF + inner, local, stride=HALF), :]
            upstream_y = jnp.where(vertical > 0, own_column(c, j - 1), own_column(c, j + 1))
            drift_x = -speed_ref[...] * (current - upstream_x)
            drift_y = -jnp.abs(vertical) * (current - upstream_y)
            column = pl.ds(c * WIDTH + j, 1)
            relaxation = rate[column, :] * (dens[column, :] * eq_ref[...] - current)
            total = current + STEP * (drift_x + drift_y + wigner + relaxation)
            slot = lax.rem(c, 2)
            result_rows[pl.ds(slot * (local * WIDTH) + j, local, stride=WIDTH), :] = total
        out_copy(c).start()

    for c in range(max(chunks - 2, 0), chunks):
        out_copy(c).wait()

    for p in range(1, groups):
        part_copy(p).wait_send()

        @pl.loop(0, chunks)
        def _(c):
            spread_copy(p, c).wait_send()

    @pl.loop(1, rows)
    def _(i):
        charge_copy(i).wait_send()

    @pl.loop(0, chunks)
    def _(c):
        @pl.when(row < rows - 1)
        def _():
            right_copy(c).wait_send()

        @pl.when(row > 0)
        def _():
            left_copy(c).wait_send()


def shards(rows, groups, distribution, region, doping, relax, equilibrium, speed, sign):
    _, local, cols, kx = distribution.shape
    modes = local * groups
    chunks = cols // WIDTH
    consts = tables(rows, groups, modes, cols)
    expand = consts[3].reshape(rows, rows, 8)
    order = (np.arange(rows)[:, None] - np.arange(rows)[None, :]) % rows
    consts[3] = np.stack([expand[:, order[r]].reshape(rows, rows * 8) for r in range(rows)])
    vmem = pl.BlockSpec(memory_space=pltpu.VMEM)
    smem = pl.BlockSpec(memory_space=pltpu.SMEM)
    hbm = pl.BlockSpec(memory_space=pl.ANY)
    piece = (local, WIDTH, kx)
    halo = (chunks, local, HALF, kx)
    dma = pltpu.SemaphoreType.DMA
    return pl.pallas_call(
        functools.partial(kernel, rows, groups),
        out_shape=jax.ShapeDtypeStruct(distribution.shape, F32),
        in_specs=[hbm, vmem, smem, smem] + [vmem] * (3 + len(consts)),
        out_specs=hbm,
        scratch_shapes=[
            pltpu.VMEM((chunks + 2,) + piece, F32),
            pltpu.VMEM((groups - 1, chunks) + piece, F32),
            pltpu.VMEM(halo, F32),
            pltpu.VMEM(halo, F32),
            pltpu.VMEM(halo, F32),
            pltpu.VMEM(halo, F32),
            pltpu.VMEM((chunks, local * WIDTH, modes), BF16),
            pltpu.VMEM((chunks, local * WIDTH, modes), BF16),
            pltpu.VMEM((cols, kx), F32),
            pltpu.VMEM((groups, 8, cols), F32),
            pltpu.VMEM((rows, 8, cols), F32),
            pltpu.VMEM((cols, modes), F32),
            pltpu.VMEM((cols, kx), F32),
            pltpu.VMEM((cols, kx), F32),
            pltpu.VMEM((2, local, HALF, kx), F32),
            pltpu.VMEM((2,) + piece, F32),
            dma((chunks,)),
            dma((groups - 1, chunks)),
            dma((groups - 1, chunks)),
            dma((groups - 1,)),
            dma((groups - 1,)),
            dma((rows - 1,)),
            dma((rows - 1,)),
            dma((chunks,)),
            dma((chunks,)),
            dma((chunks,)),
            dma((chunks,)),
            dma((2,)),
        ],
        compiler_params=pltpu.CompilerParams(
            collective_id=0, has_side_effects=True, vmem_limit_bytes=56 * 1024 * 1024
        ),
        cost_estimate=pl.CostEstimate(
            flops=2 * modes * local * cols * kx * 6,
            bytes_accessed=8 * local * cols * kx,
            transcendentals=0,
        ),
    )(
        distribution, region, doping, relax, equilibrium,
        speed.reshape(1, kx), sign.reshape(1, kx), *consts,
    )


def solution(mesh):
    return jax.shard_map(
        functools.partial(shards, mesh.shape["space"], mesh.shape["ky"]),
        mesh=mesh,
        in_specs=(
            P("space", "ky", None, None),
            P("space", None),
            P(),
            P(),
            P("ky", None),
            P(),
            P(),
        ),
        out_specs=P("space", "ky", None, None),
        check_vma=False,
    )
```

time: 390 us -> 202 us (0.52)
  Pallas kernels: 0 us -> 194 us
  blocking collectives: 166 us -> 0 us
  waiting for transfers between devices: 80.1 us -> 0 us
  local copies, waits for them, and re-layouts: 67.5 us -> 7.77 us
  other arithmetic: 29 us -> 0 us
  matrix products: 24.4 us -> 0 us
  starting transfers between devices: 21.6 us -> 0 us
    pallas_call x0 -> x1, Pallas kernels: none -> 194 us  [shards(): pl.pallas_call(functools.partial(kernel, rows, groups), out_shape=jax.Sha...]
    psum x1 -> x0, blocking collectives: 88.2 us -> none  [shards(): density = lax.psum(partial_value, 'ky')]
    all_to_all x2 -> x0, waiting for transfers between devices: 80.1 us -> none  [the longest x1 80.1 us: shards(): lax.all_to_all(mixed, 'ky', split_axis=1, concat_axis=2, tiled=True)]
    all_gather x1 -> x0, blocking collectives: 78.3 us -> none  [shards(): every_row = lax.all_gather(charge, 'space', axis=0, tiled=True)]
    dot_general x6 -> x0, matrix products: 24.4 us -> none  [the longest x1 12 us: shards(): coeffs = jnp.einsum('ab,rbm->ram', forward, flattened, precision=triple)]
    add x4 -> x0, other arithmetic: 22.3 us -> none  [the longest x1 22.3 us: shards(): return distribution + STEP * (drift_x + drift_y + wigner + relaxation)]
    all_to_all x2 -> x0, local copies, waits for them, and re-layouts: 19.5 us -> none  [the longest x1 11.8 us: shards(): lax.all_to_all(distribution, 'ky', split_axis=2, concat_axis=1, tiled=True)]
    mul x2 -> x0, local copies, waits for them, and re-layouts: 14.1 us -> none  [shards(): scaled = coeffs * jnp.concatenate([weights, weights], axis=1)[..., None]]
  transfers between devices with their start and end apart: 4 -> 0, of which waited for: 1 -> 0; matrix products, arithmetic and copies ran while one was open for 25% -> 0% of each run, Pallas kernels for 0% -> 0%
where the time goes in v1:
time: 202 us; the launch traced here: 201 us
  Pallas kernels  194 us (96%)
  local copies, waits for them, and re-layouts  7.77 us (4%)
    pallas_call x1, Pallas kernels, shards(): pl.pallas_call(functools.partial(kernel, rows, groups), out_shape=jax.Sha...  194 us
    unnamed x1, local copies, waits for them, and re-layouts  7.77 us

profile of v1, /device:TPU:0, one launch (start us, length us, event | category | flops | bytes accessed | tf_op | source)
XLA Modules:
  0.0 201.4 jit_solution(11720842513159246959)
XLA Ops:
  0.0 193.6 %shard_map.154 = f32[1,64,256,128]{3,2,1,0:T(8,128)} custom-call(f32[1,64,256,128]{3,2,1,0:T(8,128)} %f_hbm.1, s32[1,256]{1,0:T(1,128)} %region_ref.1, f32[6]{0:T(128)} %doping_ref.1, f32[6]{0:T(128)} %relax_ref.1, f32[64,128]{1,0:T(8,128)} %eq_ref.1, f32[1,128]{1,0:T(1,128)} %bitcast.2, s32[1,128]{1,0:T(1,128)} %bitcast.3, ...), custom_call_target="tpu_custom_call" | custom-call | flops 3221225472 | bytes 16777216 | tf_op jit(solution)/shard_map/pallas_call | solution.py:381
  193.6 7.8 %copy.18 = f32[1,64,256,128]{3,2,1,0:T(8,128)} copy(f32[1,64,256,128]{3,2,1,0:T(8,128)} %shard_map.154) | data formatting | bytes 16777216

commit v2 on v1

--- a/solution.py
+++ b/solution.py
@@ -15,6 +15,7 @@
 WIDTH = 16
 HALF = WIDTH // 2
 EARLY = 2
+TABLES = 9
 MESH = pl.DeviceIdType.MESH
 BF16 = jnp.bfloat16
 F32 = jnp.float32
@@ -88,17 +89,23 @@
 def kernel(
     rows, groups,
     f_hbm, region_ref, doping_ref, relax_ref, eq_ref, speed_ref, sign_ref,
-    forward_ref, backward_ref, vertical_ref, expand_ref, own_row_ref,
-    sine_ref, padded_ref, pick_ref, eigen_ref,
-    out_hbm,
-    f_vm, spread, to_left, to_right, from_left, from_right, weight_high, weight_low,
-    sums, parts, charges, diffs, dens, rate, up_x, result,
-    load_sem, spread_send, spread_recv, part_send, part_recv, charge_send, charge_recv,
-    left_send, left_recv, right_send, right_recv, out_sem,
+    *refs,
 ):
+    table_sources, out_ref, table_refs = refs[:TABLES], refs[TABLES], refs[TABLES + 1:2 * TABLES + 1]
+    (
+        forward_ref, backward_ref, vertical_ref, expand_ref, own_row_ref,
+        sine_ref, padded_ref, pick_ref, eigen_ref,
+    ) = table_refs
+    (
+        f_vm, spread, to_left, to_right, from_left, from_right, weight_high, weight_low,
+        sums, parts, charges, diffs, dens, rate, up_x,
+        load_sem, spread_send, spread_recv, part_send, part_recv, charge_send, charge_recv,
+        left_send, left_recv, right_send, right_recv, table_sem,
+    ) = refs[2 * TABLES + 1:]
     _, local, cols, kx = f_hbm.shape
     modes = local * groups
     chunks = cols // WIDTH
+    last = chunks - 1
     row = lax.axis_index("space")
     group = lax.axis_index("ky")
 
@@ -128,11 +135,16 @@
 
     pl.semaphore_wait(barrier, rows + groups - 2)
 
-    def spread_copy(p, c):
+    def spread_copy(p, c, half=None):
+        first_col = pl.multiple_of(c * WIDTH, WIDTH)
+        place, target, sem = pl.ds(first_col, WIDTH), spread.at[p - 1, c], c
+        if half is not None:
+            place = pl.ds(last * WIDTH + half * HALF, HALF)
+            target, sem = spread.at[p - 1, last, :, pl.ds(half * HALF, HALF), :], last + half
         return pltpu.make_async_remote_copy(
-            src_ref=f_hbm.at[0, :, pl.ds(pl.multiple_of(c * WIDTH, WIDTH), WIDTH), :],
-            dst_ref=spread.at[p - 1, c],
-            send_sem=spread_send.at[p - 1, c], recv_sem=spread_recv.at[p - 1, c],
+            src_ref=f_hbm.at[0, :, place, :],
+            dst_ref=target,
+            send_sem=spread_send.at[p - 1, sem], recv_sem=spread_recv.at[p - 1, sem],
             device_id=other_group(p), device_id_type=MESH,
         )
 
@@ -164,9 +176,16 @@
             device_id=other_row(rows - 1), device_id_type=MESH,
         )
 
-    for c in range(min(EARLY, chunks)):
+    for c in range(min(EARLY, last)):
         for p in range(1, groups):
             spread_copy(p, c).start()
+
+    table_copies = [
+        pltpu.make_async_copy(source, table, table_sem.at[i])
+        for i, (source, table) in enumerate(zip(table_sources, table_refs))
+    ]
+    for copy in table_copies:
+        copy.start()
 
     blank = jnp.zeros(f_vm.shape[1:], F32)
     f_vm[0] = blank
@@ -181,10 +200,14 @@
     for p in range(1, groups):
         part_copy(p).start()
 
-    @pl.loop(min(EARLY, chunks), chunks)
+    @pl.loop(min(EARLY, last), last)
     def _(c):
         for p in range(1, groups):
             spread_copy(p, c).start()
+
+    for half in range(2):
+        for p in range(1, groups):
+            spread_copy(p, last, half).start()
 
     lane = lax.broadcasted_iota(jnp.int32, (kx, kx), 1)
     place = lax.broadcasted_iota(jnp.int32, (kx, kx), 0)
@@ -250,6 +273,8 @@
             from_right[c] = jnp.zeros(from_right.shape[1:], F32)
 
     dens[...] = down(density)
+    for copy in table_copies:
+        copy.wait()
 
     @pl.loop(1, rows)
     def _(i):
@@ -279,22 +304,22 @@
     f_rows = f_vm.reshape((chunks + 2) * local * WIDTH, kx)
     spread_rows = spread.reshape((groups - 1) * chunks * local * WIDTH, kx)
     up_rows = up_x.reshape(2 * local * HALF, kx)
-    result_rows = result.reshape(2 * local * WIDTH, kx)
+    out_rows = out_ref.reshape(local * cols, kx)
+
+    def nonlocal_part(c, j, values, start):
+        count = values[0].shape[0]
+        blank_before = [jnp.zeros((start, kx), BF16)] if start else []
+        rest = modes - start - count
+        blank_after = [jnp.zeros((rest, kx), BF16)] if rest else []
+        padded = [jnp.concatenate(blank_before + [v] + blank_after, axis=0) for v in values]
+        picked = pl.ds(j * local, local)
+        return triple((weight_high[c, picked, :], weight_low[c, picked, :]), padded)
 
     def own_column(c, j):
         c, j = (c - 1, WIDTH - 1) if j < 0 else (c + 1, 0) if j == WIDTH else (c, j)
         return f_rows[pl.ds((c + 1) * (local * WIDTH) + j, local, stride=WIDTH), :]
 
-    def out_copy(c):
-        slot = lax.rem(c, 2)
-        return pltpu.make_async_copy(
-            result.at[slot],
-            out_hbm.at[0, :, pl.ds(pl.multiple_of(c * WIDTH, WIDTH), WIDTH), :],
-            out_sem.at[slot],
-        )
-
-    @pl.loop(0, chunks)
-    def _(c):
+    def advance(c, halves):
         @pl.when(row > 0)
         def _():
             right_copy(c).wait_recv()
@@ -308,25 +333,10 @@
         up_x[0] = exact(jnp.where(low_lane, left, right), first).reshape(local, HALF, kx)
         up_x[1] = exact(jnp.where(low_lane, right, left), second).reshape(local, HALF, kx)
 
-        @pl.when(c >= 2)
-        def _():
-            out_copy(c - 2).wait()
-
-        for p in range(1, groups):
-            spread_copy(p, c).wait_recv()
-
         vertical = vertical_ref[group]
         for j in range(WIDTH):
             current = own_column(c, j)
-            every = [current]
-            for p in range(groups - 1):
-                start = (p * chunks + c) * (local * WIDTH) + j
-                every.append(spread_rows[pl.ds(start, local, stride=WIDTH), :])
-            picked = pl.ds(j * local, local)
-            wigner = triple(
-                (weight_high[c, picked, :], weight_low[c, picked, :]),
-                split(jnp.concatenate(every, axis=0)),
-            )
+            wigner = nonlocal_part(c, j, list(split(current)), 0)
             half, inner = divmod(j, HALF)
             upstream_x = up_rows[pl.ds(half * local * HALF + inner, local, stride=HALF), :]
             upstream_y = jnp.where(vertical > 0, own_column(c, j - 1), own_column(c, j + 1))
@@ -335,19 +345,37 @@
             column = pl.ds(c * WIDTH + j, 1)
             relaxation = rate[column, :] * (dens[column, :] * eq_ref[...] - current)
             total = current + STEP * (drift_x + drift_y + wigner + relaxation)
-            slot = lax.rem(c, 2)
-            result_rows[pl.ds(slot * (local * WIDTH) + j, local, stride=WIDTH), :] = total
-        out_copy(c).start()
-
-    for c in range(max(chunks - 2, 0), chunks):
-        out_copy(c).wait()
+            out_rows[pl.ds(c * WIDTH + j, local, stride=cols), :] = total
+
+        for h, half in enumerate(halves):
+            for p in range(1, groups):
+                spread_copy(p, c, half).wait_recv()
+            count = WIDTH // len(halves)
+            for j in range(h * count, (h + 1) * count):
+                every = []
+                for p in range(groups - 1):
+                    start = (p * chunks + c) * (local * WIDTH) + j
+                    every.append(spread_rows[pl.ds(start, local, stride=WIDTH), :])
+                others = list(split(jnp.concatenate(every, axis=0)))
+                wigner = nonlocal_part(c, j, others, local)
+                place = pl.ds(c * WIDTH + j, local, stride=cols)
+                out_rows[place, :] = out_rows[place, :] + STEP * wigner
+
+    @pl.loop(0, last)
+    def _(c):
+        advance(c, (None,))
+
+    advance(last, (0, 1))
 
     for p in range(1, groups):
         part_copy(p).wait_send()
 
-        @pl.loop(0, chunks)
+        @pl.loop(0, last)
         def _(c):
             spread_copy(p, c).wait_send()
+
+        for half in range(2):
+            spread_copy(p, last, half).wait_send()
 
     @pl.loop(1, rows)
     def _(i):
@@ -380,10 +408,10 @@
     dma = pltpu.SemaphoreType.DMA
     return pl.pallas_call(
         functools.partial(kernel, rows, groups),
-        out_shape=jax.ShapeDtypeStruct(distribution.shape, F32),
-        in_specs=[hbm, vmem, smem, smem] + [vmem] * (3 + len(consts)),
-        out_specs=hbm,
-        scratch_shapes=[
+        out_shape=pltpu.VMEM(distribution.shape, F32),
+        in_specs=[hbm, vmem, smem, smem] + [vmem] * 3 + [hbm] * len(consts),
+        out_specs=vmem,
+        scratch_shapes=[pltpu.VMEM(t.shape, F32) for t in consts] + [
             pltpu.VMEM((chunks + 2,) + piece, F32),
             pltpu.VMEM((groups - 1, chunks) + piece, F32),
             pltpu.VMEM(halo, F32),
@@ -399,10 +427,9 @@
             pltpu.VMEM((cols, kx), F32),
             pltpu.VMEM((cols, kx), F32),
             pltpu.VMEM((2, local, HALF, kx), F32),
-            pltpu.VMEM((2,) + piece, F32),
             dma((chunks,)),
-            dma((groups - 1, chunks)),
-            dma((groups - 1, chunks)),
+            dma((groups - 1, chunks + 1)),
+            dma((groups - 1, chunks + 1)),
             dma((groups - 1,)),
             dma((groups - 1,)),
             dma((rows - 1,)),
@@ -411,10 +438,10 @@
             dma((chunks,)),
             dma((chunks,)),
             dma((chunks,)),
-            dma((2,)),
+            dma((len(consts),)),
         ],
         compiler_params=pltpu.CompilerParams(
-            collective_id=0, has_side_effects=True, vmem_limit_bytes=56 * 1024 * 1024
+            collective_id=0, has_side_effects=True, vmem_limit_bytes=52 * 1024 * 1024
         ),
         cost_estimate=pl.CostEstimate(
             flops=2 * modes * local * cols * kx * 6,

time: 202 us -> 195 us (0.965)
  local copies, waits for them, and re-layouts: 7.77 us -> 3.4 us
    unnamed x1, local copies, waits for them, and re-layouts: 7.77 us -> 3.4 us
where the time goes in v2:
time: 195 us
  Pallas kernels  192 us (98%)
  local copies, waits for them, and re-layouts  3.4 us (2%)
    pallas_call x1, Pallas kernels, shards(): pl.pallas_call(functools.partial(kernel, rows, groups), out_shape=pltpu.V...  192 us

profile of v2, /device:TPU:0, one launch (start us, length us, event | category | flops | bytes accessed | tf_op | source)
XLA Modules:
  0.0 195.2 jit_solution(10654986253295009735)
XLA Ops:
  0.0 191.7 %shard_map.154 = f32[1,64,256,128]{3,2,1,0:T(8,128)S(1)} custom-call(f32[1,64,256,128]{3,2,1,0:T(8,128)} %f_hbm.1, s32[1,256]{1,0:T(1,128)} %region_ref.1, f32[6]{0:T(128)} %doping_ref.1, f32[6]{0:T(128)} %relax_ref.1, f32[64,128]{1,0:T(8,128)} %eq_ref.1, f32[1,128]{1,0:T(1,128)} %bitcast.2, s32[1,128]{1,0:T(1,128)} %bitcast.3, ...), custom_call_target="tpu_custom_call" | custom-call | flops 3221225472 | bytes 16777216 | tf_op jit(solution)/shard_map/pallas_call | solution.py:409
  191.8 3.4 %copy.18 = f32[1,64,256,128]{3,2,1,0:T(8,128)} copy(f32[1,64,256,128]{3,2,1,0:T(8,128)S(1)} %shard_map.154) | data formatting | bytes 16777216

commit v3 on v2

--- a/solution.py
+++ b/solution.py
@@ -365,8 +365,6 @@
     def _(c):
         advance(c, (None,))
 
-    advance(last, (0, 1))
-
     for p in range(1, groups):
         part_copy(p).wait_send()
 
@@ -374,9 +372,6 @@
         def _(c):
             spread_copy(p, c).wait_send()
 
-        for half in range(2):
-            spread_copy(p, last, half).wait_send()
-
     @pl.loop(1, rows)
     def _(i):
         charge_copy(i).wait_send()
@@ -390,6 +385,12 @@
         @pl.when(row > 0)
         def _():
             left_copy(c).wait_send()
+
+    advance(last, (0, 1))
+
+    for p in range(1, groups):
+        for half in range(2):
+            spread_copy(p, last, half).wait_send()
 
 
 def shards(rows, groups, distribution, region, doping, relax, equilibrium, speed, sign):

time: 195 us -> 195 us (level)
  no operation moved by 1% of the time
where the time goes in v3:
time: 195 us
  Pallas kernels  191 us (98%)
  local copies, waits for them, and re-layouts  3.4 us (2%)
    pallas_call x1, Pallas kernels, shards(): pl.pallas_call(functools.partial(kernel, rows, groups), out_shape=pltpu.V...  191 us

profile of v3, /device:TPU:0, one launch (start us, length us, event | category | flops | bytes accessed | tf_op | source)
XLA Modules:
  0.0 194.9 jit_solution(11868731086091201711)
XLA Ops:
  0.0 191.5 %shard_map.154 = f32[1,64,256,128]{3,2,1,0:T(8,128)S(1)} custom-call(f32[1,64,256,128]{3,2,1,0:T(8,128)} %f_hbm.1, s32[1,256]{1,0:T(1,128)} %region_ref.1, f32[6]{0:T(128)} %doping_ref.1, f32[6]{0:T(128)} %relax_ref.1, f32[64,128]{1,0:T(8,128)} %eq_ref.1, f32[1,128]{1,0:T(1,128)} %bitcast.2, s32[1,128]{1,0:T(1,128)} %bitcast.3, ...), custom_call_target="tpu_custom_call" | custom-call | flops 3221225472 | bytes 16777216 | tf_op jit(solution)/shard_map/pallas_call | solution.py:410
  191.5 3.4 %copy.18 = f32[1,64,256,128]{3,2,1,0:T(8,128)} copy(f32[1,64,256,128]{3,2,1,0:T(8,128)S(1)} %shard_map.154) | data formatting | bytes 16777216
